TPU v7x, 32 devices: a whole 2x2x4 slice. The times are simulated.
32 devices in a mesh: seg: 8 (over y, x, core), row: 4 (over z).
Axes of the slice: x: 2, y: 2, z: 4, core: 2. Of those that a mesh axis runs over, the one named last changes fastest.
Arguments:
- left_env: bfloat16 [8, 512, 12, 512], P('seg', 'row'), may hold values from -4 to 4, as said below
- right_env: bfloat16 [8, 512, 12, 512], P('seg'), may hold values from -4 to 4, as said below
- site_operator: bfloat16 [4, 12, 12, 4], replicated, may hold values from -1 to 2, as said below
- start_vector: float32 [8, 512, 4, 512], P('seg', 'row'), may hold values from -6 to 6
Outputs:
- last_vector: float32 [8, 512, 4, 512], P('seg', 'row')
- alpha_values: float32 [8, 2], P('seg')
- beta_values: float32 [8, 2], P('seg')
Inputs may be any that keep to these rules, and one draw needn't show every extreme that they name: left_env[i, a, w, c] = left_env[i, c, w, a]. right_env[i, a, w, c] = right_env[i, c, w, a]. site_operator[s, v, w, r] = site_operator[r, v, w, s].
All inputs are finite; a program needn't handle non-finite values.
Results may differ from a plain program's by a relative error of at most 0.0076.
Values may be sent and summed in bfloat16 or wider, within the bound.
A program may use at most 128 MiB of HBM per device.

v0:
```python
import jax
import jax.numpy as jnp
from jax import lax
from jax.sharding import PartitionSpec as P

ITERS = 2


def passed_along(value, axis, steps):
    count = lax.axis_size(axis)
    initial, last = (max(0, -steps), min(count, count - steps))
    return lax.ppermute(value, axis, [(source, source + steps) for source in range(initial, last)])


def local(left_env, right_env, site_operator, start_vector):
    rows_here = left_env.shape[1]
    channels = left_env.shape[2]
    bond_width = left_env.shape[3]
    physical = site_operator.shape[0]
    entries = float(bond_width * physical * bond_width)
    left_local = left_env[0]
    operator_mat = site_operator.reshape(physical * channels, channels * physical)
    last_segment = lax.axis_index("seg") == lax.axis_size("seg") - 1
    received = passed_along(right_env, "seg", -1)
    right_used = jnp.where(last_segment, right_env, received)
    right_mat = right_used[0].reshape(bond_width, channels * bond_width)
    start_local = start_vector[0]
    norm_start = lax.psum(jnp.sum(start_local * start_local), "row") / entries
    current = start_local / jnp.sqrt(norm_start + 1e-06)
    previous = jnp.zeros_like(current)
    beta_prev = jnp.zeros((), jnp.float32)
    alpha_list = []
    beta_list = []
    for step_index in range(ITERS):
        lowered = current.astype(jnp.bfloat16)
        gathered = lax.all_gather(lowered, "row", axis=0, tiled=True)
        contracted = jnp.dot(
            left_local.reshape(rows_here * channels, bond_width),
            gathered.reshape(bond_width, physical * bond_width),
            preferred_element_type=jnp.float32,
        )
        contracted = contracted.astype(jnp.bfloat16).reshape(
            rows_here, channels * physical, bond_width
        )
        mixed = jnp.einsum(
            "ik,akb->aib", operator_mat, contracted, preferred_element_type=jnp.float32
        )
        mixed = mixed.astype(jnp.bfloat16).reshape(rows_here, physical, channels * bond_width)
        image = jnp.einsum("asc,bc->asb", mixed, right_mat, preferred_element_type=jnp.float32)
        image_image, image_curr, image_prev, curr_curr, prev_prev, curr_prev = lax.psum(
            (
                jnp.sum(image * image),
                jnp.sum(image * current),
                jnp.sum(image * previous),
                jnp.sum(current * current),
                jnp.sum(previous * previous),
                jnp.sum(current * previous),
            ),
            "row",
        )
        alpha = image_curr / entries
        norm_sq = (
            image_image
            - 2.0 * alpha * image_curr
            - 2.0 * beta_prev * image_prev
            + alpha * alpha * curr_curr
            + beta_prev * beta_prev * prev_prev
            + 2.0 * alpha * beta_prev * curr_prev
        ) / entries
        residual_vec = image - alpha * current - beta_prev * previous
        beta_next = jnp.sqrt(norm_sq + 1e-06)
        previous = current
        current = residual_vec / beta_next
        beta_prev = beta_next
        alpha_list.append(alpha)
        beta_list.append(beta_next)
    alpha_values = jnp.stack(alpha_list).reshape(1, ITERS)
    beta_values = jnp.stack(beta_list).reshape(1, ITERS)
    return (current[None], alpha_values, beta_values)


def solution(mesh):
    placed = (
        P("seg", "row", None, None),
        P("seg", None, None, None),
        P(),
        P("seg", "row", None, None),
    )
    return jax.shard_map(
        local,
        mesh=mesh,
        in_specs=placed,
        out_specs=(P("seg", "row", None, None), P("seg", None), P("seg", None)),
        check_vma=False,
    )
```

profile of v0, /device:TPU:0, one launch (start us, length us, event | category | flops | bytes accessed | tf_op | source)
XLA Modules:
  0.0 300.8 jit_solution(16806568525329012419)
XLA Ops:
  7.2 8.7 %copy.18 = bf16[1,512,12,512]{1,3,2,0:T(8,128)(2,1)} copy(bf16[1,512,12,512]{3,1,2,0:T(8,128)(2,1)} %param.5) | data formatting | bytes 12582912 | tf_op args[1]
  15.9 1.4 collective-permute-start
  17.4 1.1 multiply_reduce_fusion.5
  18.5 14.0 %psum.87 = f32[]{:T(128)} all-reduce(f32[]{:T(128)} %multiply_reduce_fusion.5), channel_id=1, replica_groups=mesh['seg'=8,'row'=4] {'row'}, use_global_device_ids=true, to_apply=%region_1.2 | all-reduce | flops 1 | bytes 8 | tf_op jit(solution)/shard_map/psum | solution.py:28
  33.2 1.1 bitcast_convert_fusion
  34.4 2.3 copy.13
  36.7 1.4 reshape_squeeze.7
  38.1 0.2 copy.15
  38.3 0.1 reshape.38
  38.4 41.6 %all-gather.3.cloned.1.call-done = bf16[512,4,512]{2,0,1:T(8,128)(2,1)} async-done(((bf16[128,4,512]{2,0,1:T(8,128)(2,1)}), bf16[512,4,512]{2,0,1:T(8,128)(2,1)}) %all-gather.3.cloned.1.call-update) | async-done | bytes 2097168 | tf_op jit(solution)/shard_map/all_gather | solution.py:36
  80.0 2.8 copy.12
  82.8 6.8 %fusion = bf16[1536,2048]{0,1:T(8,128)(2,1)} fusion(bf16[512,2048]{0,1:T(8,128)(2,1)S(1)} %bitcast.73, bf16[1536,512]{1,0:T(8,128)(2,1)} %reshape_squeeze.7), kind=kOutput, calls=%fused_computation.2 | convolution fusion | flops 3224371200 | bytes 9961472 | tf_op jit(solution)/shard_map/dot_general | solution.py:37
  89.6 8.6 %copy.14 = bf16[1536,2048]{1,0:T(8,128)(2,1)} copy(bf16[1536,2048]{0,1:T(8,128)(2,1)} %fusion) | data formatting | bytes 12582912 | tf_op jit(solution)/shard_map/convert_element_type | solution.py:42
  98.2 10.7 %reshape.37 = bf16[128,48,512]{2,1,0:T(8,128)(2,1)} reshape(bf16[1536,2048]{1,0:T(8,128)(2,1)} %copy.14) | data formatting | bytes 12582912 | tf_op jit(solution)/shard_map/reshape | solution.py:42
  108.9 7.3 %convert_bitcast_fusion.1 = bf16[128,48,512]{2,1,0:T(8,128)(2,1)} fusion(bf16[128,48,512]{2,1,0:T(8,128)(2,1)} %reshape.37, bf16[48,48]{0,1:T(8,128)(2,1)S(1)} %reshape.38), kind=kOutput, calls=%fused_computation.9 | convolution fusion | flops 305135616 | bytes 12587520 | tf_op jit(solution)/shard_map/ik,akb->aib/dot_general | solution.py:45
  116.2 13.6 %reshape.39 = bf16[128,4,6144]{2,1,0:T(4,128)(2,1)} reshape(bf16[128,48,512]{2,1,0:T(8,128)(2,1)} %convert_bitcast_fusion.1) | data formatting | bytes 12582912 | tf_op jit(solution)/shard_map/reshape | solution.py:48
  129.8 6.1 %broadcast_select_fusion = bf16[1,512,12,512]{1,3,2,0:T(8,128)(2,1)} fusion(bf16[1,512,12,512]{1,3,2,0:T(8,128)(2,1)} %copy.18, bf16[1,512,12,512]{1,3,2,0:T(8,128)(2,1)} %collective-permute-done, pred[]{:T(512)S(6)} %eq.3), kind=kLoop, calls=%fused_computation.10 | loop fusion | flops 3145728 | bytes 18874368 | tf_op jit(solution)/shard_map/jit(_where)/select_n | solution.py:25
  135.9 11.5 %fusion.10 = (f32[]{:T(128)}, f32[]{:T(128)}, f32[]{:T(128)}, f32[]{:T(128)}, f32[]{:T(128)}, /*index=5*/f32[128,4,512]{2,0,1:T(8,128)S(1)}) fusion(f32[]{:T(128)S(6)} %sqrt.9, f32[1,128,4,512]{3,2,1,0:T(4,128)S(1)} %copy-done, bf16[512,6144,1]{0,1,2:T(8,128)(2,1)} %bitcast.70, bf16[128,4,6144]{2,1,0:T(4,128)(2,1)} %reshape.39), kind=kOutput, calls=%fused_computation.23 | convolution fusion | flops 3224109056 | bytes 14680088 | tf_op jit(solution)/shard_map/asc,bc->asb/dot_general | solution.py:49
  147.4 10.9 %all-reduce.1 = (f32[]{:T(128)}, f32[]{:T(128)}, f32[]{:T(128)}, f32[]{:T(128)}, f32[]{:T(128)}, /*index=5*/f32[]{:T(128)}) all-reduce(f32[]{:T(128)} %get-tuple-element.18, f32[]{:T(128)} %get-tuple-element.16, f32[]{:T(128)} %get-tuple-element.17, f32[]{:T(128)} %get-tuple-element.15, ...), channel_id=1, replica_groups=mesh['seg'=8,'row'=4] {'row'}, use_global_device_ids=true, to_apply=%region_5.6 | all-reduce | flops 6 | bytes 48 | tf_op jit(solution)/shard_map/psum | solution.py:50
  165.4 1.2 fusion.18
  167.3 43.9 %all-gather.5.cloned.1.call-done = bf16[512,4,512]{2,0,1:T(8,128)(2,1)} async-done(((bf16[128,4,512]{2,0,1:T(8,128)(2,1)}), bf16[512,4,512]{2,0,1:T(8,128)(2,1)}) %all-gather.5.cloned.1.call-update) | async-done | bytes 2097168 | tf_op jit(solution)/shard_map/all_gather | solution.py:36
  211.2 4.2 %copy.21 = bf16[512,4,512]{0,2,1:T(8,128)(2,1)} copy(bf16[512,4,512]{2,0,1:T(8,128)(2,1)} %all-gather.5.cloned.1.call-done) | data formatting | bytes 4194304 | tf_op jit(solution)/shard_map/all_gather | solution.py:36
  215.3 8.2 %fusion.1 = bf16[1536,2048]{0,1:T(8,128)(2,1)} fusion(bf16[512,2048]{0,1:T(8,128)(2,1)} %bitcast.72, bf16[1536,512]{1,0:T(8,128)(2,1)} %reshape_squeeze.7), kind=kOutput, calls=%fused_computation.3 | convolution fusion | flops 3224371200 | bytes 9961472 | tf_op jit(solution)/shard_map/dot_general | solution.py:37
  223.5 8.6 %copy.22 = bf16[1536,2048]{1,0:T(8,128)(2,1)} copy(bf16[1536,2048]{0,1:T(8,128)(2,1)} %fusion.1) | data formatting | bytes 12582912 | tf_op jit(solution)/shard_map/convert_element_type | solution.py:42
  232.1 10.7 %reshape.41 = bf16[128,48,512]{2,1,0:T(8,128)(2,1)} reshape(bf16[1536,2048]{1,0:T(8,128)(2,1)} %copy.22) | data formatting | bytes 12582912 | tf_op jit(solution)/shard_map/reshape | solution.py:42
  242.8 7.2 %convert_bitcast_fusion = bf16[128,48,512]{2,1,0:T(8,128)(2,1)} fusion(bf16[128,48,512]{2,1,0:T(8,128)(2,1)} %reshape.41, bf16[48,48]{0,1:T(8,128)(2,1)S(1)} %reshape.38), kind=kOutput, calls=%fused_computation.8 | convolution fusion | flops 305135616 | bytes 12587520 | tf_op jit(solution)/shard_map/ik,akb->aib/dot_general | solution.py:45
  250.0 13.6 %reshape.42 = bf16[128,4,6144]{2,1,0:T(4,128)(2,1)} reshape(bf16[128,48,512]{2,1,0:T(8,128)(2,1)} %convert_bitcast_fusion) | data formatting | bytes 12582912 | tf_op jit(solution)/shard_map/reshape | solution.py:48
  263.6 11.5 %fusion.15 = (f32[]{:T(128)}, f32[]{:T(128)}, f32[]{:T(128)}, f32[]{:T(128)}, f32[]{:T(128)}, /*index=5*/f32[128,4,512]{2,0,1:T(8,128)S(1)}) fusion(f32[128,4,512]{2,0,1:T(8,128)S(1)} %get-tuple-element.31, f32[]{:T(128)S(6)} %sqrt.9, f32[1,128,4,512]{3,2,1,0:T(4,128)S(1)} %copy-done, bf16[512,6144,1]{0,1,2:T(8,128)(2,1)} %bitcast.71, ...), kind=kOutput, calls=%fused_computation.28 | convolution fusion | flops 3224109056 | bytes 15728664 | tf_op jit(solution)/shard_map/asc,bc->asb/dot_general | solution.py:49
  275.1 10.2 %all-reduce = (f32[]{:T(128)}, f32[]{:T(128)}, f32[]{:T(128)}, f32[]{:T(128)}, f32[]{:T(128)}) all-reduce(f32[]{:T(128)} %get-tuple-element.12, f32[]{:T(128)} %get-tuple-element.11, f32[]{:T(128)} %get-tuple-element.10, f32[]{:T(128)} %get-tuple-element.13, f32[]{:T(128)} %get-tuple-element.9), channel_id=1, replica_groups=mesh['seg'=8,'row'=4] {'row'}, use_global_device_ids=true, to_apply=%region_16.17 | all-reduce | flops 5 | bytes 40 | tf_op jit(solution)/shard_map/psum | solution.py:50
  291.2 0.5 fusion.13
  291.7 1.6 copy.26
  293.3 0.6 maximum_bitcast_fusion
  (9 shorter events, 0.1 us)
Async XLA Ops:
  7.2 10.2 %copy-start = (f32[1,128,4,512]{3,2,1,0:T(4,128)S(1)}, f32[1,128,4,512]{3,2,1,0:T(4,128)}, u32[]{:S(2)}) copy-start(f32[1,128,4,512]{3,2,1,0:T(4,128)} %param.7) | copy-start | bytes 3145732
  7.2 72.9 %all-gather.3.cloned.1.call-start = ((), (), s32[]{:S(2)}) async-start(), calls=%async_computation | async-start | bytes 2621440 | tf_op jit(solution)/shard_map/all_gather | solution.py:36
  15.9 22.1 %copy-start.1 = (bf16[4,12,12,4]{2,3,1,0:T(4,128)(2,1)S(1)}, bf16[4,12,12,4]{2,3,1,0:T(4,128)(2,1)}, u32[]{:S(2)}) copy-start(bf16[4,12,12,4]{2,3,1,0:T(4,128)(2,1)} %param.6) | copy-start | bytes 13828
  15.9 113.9 %collective-permute-start = (bf16[1,512,12,512]{1,3,2,0:T(8,128)(2,1)}, bf16[1,512,12,512]{1,3,2,0:T(8,128)(2,1)}, u32[]{:S(2)}, u32[]{:S(2)}) collective-permute-start(bf16[1,512,12,512]{1,3,2,0:T(8,128)(2,1)} %copy.18), channel_id=1, source_target_pairs={{4,0},{8,4},{12,8},{16,12},{20,16},{24,20},{28,24},{5,1},{9,5},{13... | collective-permute-start | bytes 18874376 | tf_op jit(solution)/shard_map/ppermute | solution.py:12
  34.3 176.8 %all-gather.5.cloned.1.call-start = ((), (), s32[]{:S(2)}) async-start(), calls=%async_computation.1 | async-start | bytes 2621440 | tf_op jit(solution)/shard_map/all_gather | solution.py:36
Sparse Core Ops, SparseCore 0:
  34.4 45.5 all-gather.2
  166.7 44.3 all-gather.4
where the time goes:
time: 303 us; the launch traced here: 301 us
  local copies, waits for them, and re-layouts  87.1 us (29%)
  waiting for transfers between devices  85.5 us (28%)
  matrix products  52.4 us (17%)
  blocking collectives  35.1 us (12%)
  between operations  28.4 us (9%)
  other arithmetic  10.6 us (3%)
    all_gather x2, waiting for transfers between devices, local(): gathered = lax.all_gather(lowered, 'row', axis=0, tiled=True)  85.5 us
    reshape x2, local copies, waits for them, and re-layouts, local(): mixed.astype(jnp.bfloat16)  27.2 us
    dot_general x2, matrix products, local(): jnp.einsum('asc,bc->asb', mixed, right_mat, preferred_element_type=jnp.fl...  22.9 us
    reshape x2, local copies, waits for them, and re-layouts, local(): contracted.astype(jnp.bfloat16)  21.4 us
    psum x2, blocking collectives, local(): lax.psum((jnp.sum(image * image), jnp.sum(image * current), jnp.sum(image...  21.1 us
    convert_element_type x2, local copies, waits for them, and re-layouts, local(): contracted.astype(jnp.bfloat16)  17.2 us
    dot_general x2, matrix products, local(): jnp.dot(left_local.reshape(rows_here * channels, bond_width), gathered.re...  14.9 us
    dot_general x2, matrix products, local(): jnp.einsum('ik,akb->aib', operator_mat, contracted, preferred_element_typ...  14.6 us
  transfers between devices with their start and end apart: 3, of which 2 were waited for; matrix products, arithmetic and copies ran while one was open for 19% of the time, Pallas kernels for 0%

commit v1 on v0

--- a/solution.py
+++ b/solution.py
@@ -4,6 +4,22 @@
 from jax.sharding import PartitionSpec as P
 
 ITERS = 2
+
+
+def collect(x, axis, dim):
+    ways, here, step = (lax.axis_size(axis), lax.axis_index(axis), x.shape[dim])
+    dims = [n * ways if d == dim else n for d, n in enumerate(x.shape)]
+    full = lax.dynamic_update_slice_in_dim(jnp.zeros(dims, x.dtype), x, here * step, axis=dim)
+    going_up = going_down = x
+    for far in range(1, ways // 2 + 1):
+        going_up = lax.ppermute(going_up, axis, [(d, (d + 1) % ways) for d in range(ways)])
+        full = lax.dynamic_update_slice_in_dim(full, going_up, (here - far) % ways * step, axis=dim)
+        if 2 * far < ways:
+            going_down = lax.ppermute(going_down, axis, [(d, (d - 1) % ways) for d in range(ways)])
+            full = lax.dynamic_update_slice_in_dim(
+                full, going_down, (here + far) % ways * step, axis=dim
+            )
+    return full
 
 
 def passed_along(value, axis, steps):
@@ -33,7 +49,7 @@
     beta_list = []
     for step_index in range(ITERS):
         lowered = current.astype(jnp.bfloat16)
-        gathered = lax.all_gather(lowered, "row", axis=0, tiled=True)
+        gathered = collect(lowered, "row", 0)
         contracted = jnp.dot(
             left_local.reshape(rows_here * channels, bond_width),
             gathered.reshape(bond_width, physical * bond_width),

time: 303 us -> 274 us (0.904); the launches traced: 301 us -> 268 us
  waiting for transfers between devices: 85.5 us -> 41.2 us
  local copies, waits for them, and re-layouts: 87.1 us -> 102 us
  between operations: 28.4 us -> 14.8 us
  starting transfers between devices: 1.49 us -> 11.9 us
    all_gather x2 -> x0, waiting for transfers between devices: 85.5 us -> none  [local(): gathered = lax.all_gather(lowered, 'row', axis=0, tiled=True)]
    ppermute x0 -> x6, waiting for transfers between devices: none -> 41.2 us  [the longest x4 39.4 us: collect(): lax.ppermute(going_up, axis, [(d, (d + 1) % ways) for d in range(ways)])]
    ppermute x0 -> x6, starting transfers between devices: none -> 10.5 us  [the longest x2 5.68 us: collect(): lax.ppermute(going_down, axis, [(d, (d - 1) % ways) for d in range(ways)])]
    ppermute x0 -> x6, local copies, waits for them, and re-layouts: none -> 10 us  [the longest x4 6.7 us: collect(): lax.ppermute(going_up, axis, [(d, (d + 1) % ways) for d in range(ways)])]
    dynamic_update_slice x0 -> x8, local copies, waits for them, and re-layouts: none -> 8.16 us  [the longest x4 4.09 us: collect(): lax.dynamic_update_slice_in_dim(full, going_up, (here - far) % ways * ste...]
    all_gather x2 -> x0, local copies, waits for them, and re-layouts: 6.95 us -> none  [local(): gathered = lax.all_gather(lowered, 'row', axis=0, tiled=True)]
  transfers between devices with their start and end apart: 3 -> 7, of which waited for: 2 -> 5; matrix products, arithmetic and copies ran while one was open for 19% -> 27% of each run, Pallas kernels for 0% -> 0%
where the time goes in v1:
time: 274 us; the launch traced here: 268 us
  local copies, waits for them, and re-layouts  102 us (37%)
  matrix products  54.4 us (20%)
  waiting for transfers between devices  41.2 us (15%)
  blocking collectives  32.7 us (12%)
  between operations  14.8 us (5%)
  starting transfers between devices  11.9 us (4%)
  other arithmetic  11 us (4%)
    ppermute x4, waiting for transfers between devices, collect(): lax.ppermute(going_up, axis, [(d, (d + 1) % ways) for d in range(ways)])  39.4 us
    reshape x2, local copies, waits for them, and re-layouts, local(): mixed.astype(jnp.bfloat16)  27.2 us
    dot_general x2, matrix products, local(): jnp.einsum('asc,bc->asb', mixed, right_mat, preferred_element_type=jnp.fl...  24.9 us
    reshape x2, local copies, waits for them, and re-layouts, local(): contracted.astype(jnp.bfloat16)  21.4 us
    psum x2, blocking collectives, local(): lax.psum((jnp.sum(image * image), jnp.sum(image * current), jnp.sum(image...  18.7 us
    convert_element_type x2, local copies, waits for them, and re-layouts, local(): contracted.astype(jnp.bfloat16)  17.2 us
    dot_general x2, matrix products, local(): jnp.dot(left_local.reshape(rows_here * channels, bond_width), gathered.re...  14.9 us
    dot_general x2, matrix products, local(): jnp.einsum('ik,akb->aib', operator_mat, contracted, preferred_element_typ...  14.6 us
  transfers between devices with their start and end apart: 7, of which 5 were waited for; matrix products, arithmetic and copies ran while one was open for 27% of the time, Pallas kernels for 0%

profile of v1, /device:TPU:0, one launch (start us, length us, event | category | flops | bytes accessed | tf_op | source)
XLA Modules:
  0.0 268.4 jit_solution(9812573151616192616)
XLA Ops:
  0.6 8.7 %copy.21 = bf16[1,512,12,512]{1,3,2,0:T(8,128)(2,1)} copy(bf16[1,512,12,512]{3,1,2,0:T(8,128)(2,1)} %param.5) | data formatting | bytes 12582912 | tf_op args[1]
  11.9 14.0 %psum.87 = f32[]{:T(128)} all-reduce(f32[]{:T(128)} %multiply_reduce_fusion.5), channel_id=1, replica_groups=mesh['seg'=8,'row'=4] {'row'}, use_global_device_ids=true, to_apply=%region_1.2 | all-reduce | flops 1 | bytes 8 | tf_op jit(solution)/shard_map/psum | solution.py:44
  27.7 3.8 %collective-permute-start.1 = (bf16[128,4,512]{2,0,1:T(8,128)(2,1)}, bf16[128,4,512]{2,0,1:T(8,128)(2,1)}, u32[]{:S(2)}, u32[]{:S(2)}) collective-permute-start(bf16[128,4,512]{2,0,1:T(8,128)(2,1)} %bitcast_convert_fusion), channel_id=1, source_target_pairs={{0,3},{1,0},{2,1},{3,2},{4,7},{5,4},{6,5},{7,6},{8,11},{9,8},{10,9... | collective-permute-start | bytes 1572872 | tf_op jit(solution)/shard_map/ppermute | solution.py:18
  31.6 13.2 %collective-permute-done = bf16[128,4,512]{2,0,1:T(8,128)(2,1)} collective-permute-done((bf16[128,4,512]{2,0,1:T(8,128)(2,1)}, bf16[128,4,512]{2,0,1:T(8,128)(2,1)}, u32[]{:S(2)}, u32[]{:S(2)}) %collective-permute-start) | collective-permute-done | bytes 524320 | tf_op jit(solution)/shard_map/ppermute | solution.py:15
  44.7 2.0 copy.12
  46.8 2.3 copy.16
  52.1 2.0 copy.13
  54.2 2.0 copy.14
  58.6 6.9 %collective-permute-done.2 = bf16[128,4,512]{2,0,1:T(8,128)(2,1)} collective-permute-done((bf16[128,4,512]{2,0,1:T(8,128)(2,1)}, bf16[128,4,512]{2,0,1:T(8,128)(2,1)}, u32[]{:S(2)}, u32[]{:S(2)}) %collective-permute-start.2) | collective-permute-done | bytes 524320 | tf_op jit(solution)/shard_map/ppermute | solution.py:15
  65.4 2.0 copy.15
  68.6 6.7 %fusion = bf16[1536,2048]{0,1:T(8,128)(2,1)} fusion(bf16[512,2048]{0,1:T(8,128)(2,1)S(1)} %bitcast.72, bf16[1536,512]{1,0:T(8,128)(2,1)} %reshape_squeeze.7), kind=kOutput, calls=%fused_computation.2 | convolution fusion | flops 3224371200 | bytes 9961472 | tf_op jit(solution)/shard_map/dot_general | solution.py:53
  75.4 8.6 %copy.17 = bf16[1536,2048]{1,0:T(8,128)(2,1)} copy(bf16[1536,2048]{0,1:T(8,128)(2,1)} %fusion) | data formatting | bytes 12582912 | tf_op jit(solution)/shard_map/convert_element_type | solution.py:58
  84.0 10.7 %reshape.37 = bf16[128,48,512]{2,1,0:T(8,128)(2,1)} reshape(bf16[1536,2048]{1,0:T(8,128)(2,1)} %copy.17) | data formatting | bytes 12582912 | tf_op jit(solution)/shard_map/reshape | solution.py:58
  94.7 7.3 %convert_bitcast_fusion.1 = bf16[128,48,512]{2,1,0:T(8,128)(2,1)} fusion(bf16[128,48,512]{2,1,0:T(8,128)(2,1)} %reshape.37, bf16[48,48]{0,1:T(8,128)(2,1)S(1)} %reshape.38), kind=kOutput, calls=%fused_computation.9 | convolution fusion | flops 305135616 | bytes 12587520 | tf_op jit(solution)/shard_map/ik,akb->aib/dot_general | solution.py:61
  102.0 13.6 %reshape.39 = bf16[128,4,6144]{2,1,0:T(4,128)(2,1)} reshape(bf16[128,48,512]{2,1,0:T(8,128)(2,1)} %convert_bitcast_fusion.1) | data formatting | bytes 12582912 | tf_op jit(solution)/shard_map/reshape | solution.py:64
  115.6 6.1 %broadcast_select_fusion = bf16[1,512,12,512]{1,3,2,0:T(8,128)(2,1)} fusion(bf16[1,512,12,512]{1,3,2,0:T(8,128)(2,1)} %copy.21, bf16[1,512,12,512]{1,3,2,0:T(8,128)(2,1)} %collective-permute-done.3, pred[]{:T(512)S(6)} %eq.10), kind=kLoop, calls=%fused_computation.10 | loop fusion | flops 3145728 | bytes 18874368 | tf_op jit(solution)/shard_map/jit(_where)/select_n | solution.py:41
  121.7 13.5 %fusion.10 = (f32[]{:T(128)}, f32[]{:T(128)}, f32[]{:T(128)}, f32[]{:T(128)}, f32[]{:T(128)}, /*index=5*/f32[128,4,512]{2,0,1:T(8,128)}) fusion(f32[]{:T(128)S(6)} %sqrt.9, f32[1,128,4,512]{3,2,1,0:T(4,128)S(1)} %copy-done, bf16[512,6144,1]{0,1,2:T(8,128)(2,1)} %bitcast.70, bf16[128,4,6144]{2,1,0:T(4,128)(2,1)} %reshape.39), kind=kOutput, calls=%fused_computation.23 | convolution fusion | flops 3224109056 | bytes 14680088 | tf_op jit(solution)/shard_map/asc,bc->asb/dot_general | solution.py:65
  135.2 9.6 %all-reduce.1 = (f32[]{:T(128)}, f32[]{:T(128)}, f32[]{:T(128)}, f32[]{:T(128)}, f32[]{:T(128)}, /*index=5*/f32[]{:T(128)}) all-reduce(f32[]{:T(128)} %get-tuple-element.18, f32[]{:T(128)} %get-tuple-element.16, f32[]{:T(128)} %get-tuple-element.17, f32[]{:T(128)} %get-tuple-element.15, ...), channel_id=1, replica_groups=mesh['seg'=8,'row'=4] {'row'}, use_global_device_ids=true, to_apply=%region_5.6 | all-reduce | flops 6 | bytes 48 | tf_op jit(solution)/shard_map/psum | solution.py:66
  153.2 2.0 collective-permute-start.4
  155.2 1.9 collective-permute-start.5
  157.1 12.9 %collective-permute-done.4 = bf16[128,4,512]{2,0,1:T(8,128)(2,1)} collective-permute-done((bf16[128,4,512]{2,0,1:T(8,128)(2,1)S(1)}, bf16[128,4,512]{2,0,1:T(8,128)(2,1)}, u32[]{:S(2)}, u32[]{:S(2)}) %collective-permute-start.4) | collective-permute-done | bytes 524320 | tf_op jit(solution)/shard_map/ppermute | solution.py:15
  170.0 2.8 %collective-permute-start.6 = (bf16[128,4,512]{2,0,1:T(8,128)(2,1)}, bf16[128,4,512]{2,0,1:T(8,128)(2,1)}, u32[]{:S(2)}, u32[]{:S(2)}) collective-permute-start(bf16[128,4,512]{2,0,1:T(8,128)(2,1)} %collective-permute-done.4), channel_id=1, source_target_pairs={{0,1},{1,2},{2,3},{3,0},{4,5},{5,6},{6,7},{7,4},{8,9},{9,10},{10,1... | collective-permute-start | bytes 1572872 | tf_op jit(solution)/shard_map/ppermute | solution.py:15
  177.4 1.8 collective-permute-done.5
  182.3 6.4 %collective-permute-done.6 = bf16[128,4,512]{2,0,1:T(8,128)(2,1)} collective-permute-done((bf16[128,4,512]{2,0,1:T(8,128)(2,1)}, bf16[128,4,512]{2,0,1:T(8,128)(2,1)}, u32[]{:S(2)}, u32[]{:S(2)}) %collective-permute-start.6) | collective-permute-done | bytes 524320 | tf_op jit(solution)/shard_map/ppermute | solution.py:15
  190.9 8.2 %fusion.1 = bf16[1536,2048]{0,1:T(8,128)(2,1)} fusion(bf16[512,2048]{0,1:T(8,128)(2,1)} %bitcast.7, bf16[1536,512]{1,0:T(8,128)(2,1)} %reshape_squeeze.7), kind=kOutput, calls=%fused_computation.3 | convolution fusion | flops 3224371200 | bytes 9961472 | tf_op jit(solution)/shard_map/dot_general | solution.py:53
  199.1 8.6 %copy.28 = bf16[1536,2048]{1,0:T(8,128)(2,1)} copy(bf16[1536,2048]{0,1:T(8,128)(2,1)} %fusion.1) | data formatting | bytes 12582912 | tf_op jit(solution)/shard_map/convert_element_type | solution.py:58
  207.7 10.7 %reshape.41 = bf16[128,48,512]{2,1,0:T(8,128)(2,1)} reshape(bf16[1536,2048]{1,0:T(8,128)(2,1)} %copy.28) | data formatting | bytes 12582912 | tf_op jit(solution)/shard_map/reshape | solution.py:58
  218.4 7.2 %convert_bitcast_fusion = bf16[128,48,512]{2,1,0:T(8,128)(2,1)} fusion(bf16[128,48,512]{2,1,0:T(8,128)(2,1)} %reshape.41, bf16[48,48]{0,1:T(8,128)(2,1)S(1)} %reshape.38), kind=kOutput, calls=%fused_computation.8 | convolution fusion | flops 305135616 | bytes 12587520 | tf_op jit(solution)/shard_map/ik,akb->aib/dot_general | solution.py:61
  225.7 13.6 %reshape.42 = bf16[128,4,6144]{2,1,0:T(4,128)(2,1)} reshape(bf16[128,48,512]{2,1,0:T(8,128)(2,1)} %convert_bitcast_fusion) | data formatting | bytes 12582912 | tf_op jit(solution)/shard_map/reshape | solution.py:64
  239.2 11.5 %fusion.15 = (f32[]{:T(128)}, f32[]{:T(128)}, f32[]{:T(128)}, f32[]{:T(128)}, f32[]{:T(128)}, /*index=5*/f32[128,4,512]{2,0,1:T(8,128)S(1)}) fusion(f32[128,4,512]{2,0,1:T(8,128)S(1)} %get-tuple-element.31, f32[]{:T(128)S(6)} %sqrt.9, f32[1,128,4,512]{3,2,1,0:T(4,128)S(1)} %copy-done, bf16[512,6144,1]{0,1,2:T(8,128)(2,1)} %bitcast.71, ...), kind=kOutput, calls=%fused_computation.28 | convolution fusion | flops 3224109056 | bytes 15728664 | tf_op jit(solution)/shard_map/asc,bc->asb/dot_general | solution.py:65
  250.7 9.1 %all-reduce = (f32[]{:T(128)}, f32[]{:T(128)}, f32[]{:T(128)}, f32[]{:T(128)}, f32[]{:T(128)}) all-reduce(f32[]{:T(128)} %get-tuple-element.12, f32[]{:T(128)} %get-tuple-element.11, f32[]{:T(128)} %get-tuple-element.10, f32[]{:T(128)} %get-tuple-element.13, f32[]{:T(128)} %get-tuple-element.9), channel_id=1, replica_groups=mesh['seg'=8,'row'=4] {'row'}, use_global_device_ids=true, to_apply=%region_16.17 | all-reduce | flops 5 | bytes 40 | tf_op jit(solution)/shard_map/psum | solution.py:66
  266.2 1.6 copy.32
  (31 shorter events, 22.1 us)
Async XLA Ops:
  0.6 10.2 %copy-start = (f32[1,128,4,512]{3,2,1,0:T(4,128)S(1)}, f32[1,128,4,512]{3,2,1,0:T(4,128)}, u32[]{:S(2)}) copy-start(f32[1,128,4,512]{3,2,1,0:T(4,128)} %param.7) | copy-start | bytes 3145732
  9.4 41.1 %copy-start.1 = (bf16[4,12,12,4]{2,3,1,0:T(4,128)(2,1)S(1)}, bf16[4,12,12,4]{2,3,1,0:T(4,128)(2,1)}, u32[]{:S(2)}) copy-start(bf16[4,12,12,4]{2,3,1,0:T(4,128)(2,1)} %param.6) | copy-start | bytes 13828
  9.4 106.3 %collective-permute-start.3 = (bf16[1,512,12,512]{1,3,2,0:T(8,128)(2,1)}, bf16[1,512,12,512]{1,3,2,0:T(8,128)(2,1)}, u32[]{:S(2)}, u32[]{:S(2)}) collective-permute-start(bf16[1,512,12,512]{1,3,2,0:T(8,128)(2,1)} %copy.21), channel_id=1, source_target_pairs={{4,0},{8,4},{12,8},{16,12},{20,16},{24,20},{28,24},{5,1},{9,5},{13... | collective-permute-start | bytes 18874376 | tf_op jit(solution)/shard_map/ppermute | solution.py:28
  27.7 17.0 %collective-permute-start = (bf16[128,4,512]{2,0,1:T(8,128)(2,1)}, bf16[128,4,512]{2,0,1:T(8,128)(2,1)}, u32[]{:S(2)}, u32[]{:S(2)}) collective-permute-start(bf16[128,4,512]{2,0,1:T(8,128)(2,1)} %bitcast_convert_fusion), channel_id=1, source_target_pairs={{0,1},{1,2},{2,3},{3,0},{4,5},{5,6},{6,7},{7,4},{8,9},{9,10},{10,1... | collective-permute-start | bytes 1572872 | tf_op jit(solution)/shard_map/ppermute | solution.py:15
  27.7 26.4 %collective-permute-start.1 = (bf16[128,4,512]{2,0,1:T(8,128)(2,1)}, bf16[128,4,512]{2,0,1:T(8,128)(2,1)}, u32[]{:S(2)}, u32[]{:S(2)}) collective-permute-start(bf16[128,4,512]{2,0,1:T(8,128)(2,1)} %bitcast_convert_fusion), channel_id=1, source_target_pairs={{0,3},{1,0},{2,1},{3,2},{4,7},{5,4},{6,5},{7,6},{8,11},{9,8},{10,9... | collective-permute-start | bytes 1572872 | tf_op jit(solution)/shard_map/ppermute | solution.py:18
  44.7 20.7 %collective-permute-start.2 = (bf16[128,4,512]{2,0,1:T(8,128)(2,1)}, bf16[128,4,512]{2,0,1:T(8,128)(2,1)}, u32[]{:S(2)}, u32[]{:S(2)}) collective-permute-start(bf16[128,4,512]{2,0,1:T(8,128)(2,1)} %collective-permute-done), channel_id=1, source_target_pairs={{0,1},{1,2},{2,3},{3,0},{4,5},{5,6},{6,7},{7,4},{8,9},{9,10},{10,1... | collective-permute-start | bytes 1572872 | tf_op jit(solution)/shard_map/ppermute | solution.py:15
  153.2 16.8 %collective-permute-start.4 = (bf16[128,4,512]{2,0,1:T(8,128)(2,1)S(1)}, bf16[128,4,512]{2,0,1:T(8,128)(2,1)}, u32[]{:S(2)}, u32[]{:S(2)}) collective-permute-start(bf16[128,4,512]{2,0,1:T(8,128)(2,1)S(1)} %get-tuple-element.30), channel_id=1, source_target_pairs={{0,1},{1,2},{2,3},{3,0},{4,5},{5,6},{6,7},{7,4},{8,9},{9,10},{10,1... | collective-permute-start | bytes 1572872 | tf_op jit(solution)/shard_map/ppermute | solution.py:15
  155.2 24.0 %collective-permute-start.5 = (bf16[128,4,512]{2,0,1:T(8,128)(2,1)S(1)}, bf16[128,4,512]{2,0,1:T(8,128)(2,1)}, u32[]{:S(2)}, u32[]{:S(2)}) collective-permute-start(bf16[128,4,512]{2,0,1:T(8,128)(2,1)S(1)} %get-tuple-element.30), channel_id=1, source_target_pairs={{0,3},{1,0},{2,1},{3,2},{4,7},{5,4},{6,5},{7,6},{8,11},{9,8},{10,9... | collective-permute-start | bytes 1572872 | tf_op jit(solution)/shard_map/ppermute | solution.py:18
  170.0 18.7 %collective-permute-start.6 = (bf16[128,4,512]{2,0,1:T(8,128)(2,1)}, bf16[128,4,512]{2,0,1:T(8,128)(2,1)}, u32[]{:S(2)}, u32[]{:S(2)}) collective-permute-start(bf16[128,4,512]{2,0,1:T(8,128)(2,1)} %collective-permute-done.4), channel_id=1, source_target_pairs={{0,1},{1,2},{2,3},{3,0},{4,5},{5,6},{6,7},{7,4},{8,9},{9,10},{10,1... | collective-permute-start | bytes 1572872 | tf_op jit(solution)/shard_map/ppermute | solution.py:15
